TPU v7x, 32 devices: a whole 2x2x4 slice. The times are simulated.
32 devices in a mesh: energy: 8 (over z, y), momentum: 4 (over x, core).
Axes of the slice: x: 2, y: 2, z: 4, core: 2. Of those that a mesh axis runs over, the one named last changes fastest.
Arguments:
- lesser: bfloat16 [8, 4, 2, 512, 512], P('energy', 'momentum'), may hold values from -6 to 6
- greater: bfloat16 [8, 4, 2, 512, 512], P('energy', 'momentum'), may hold values from -6 to 6
- retarded: bfloat16 [8, 4, 2, 512, 512], P('energy', 'momentum'), may hold values from -4.1875 to 4.1875
- occupation: float32 [2], replicated, may hold values from 0.1 to 2
- shift_slots: int32 [2, 2, 8], replicated, may hold values from 0 to 8, as said below
- coupling: int32 [2, 4, 4], replicated, may hold values from 1 to 8
Outputs:
- lesser_new: bfloat16 [8, 4, 2, 512, 512], P('energy', 'momentum')
- greater_new: bfloat16 [8, 4, 2, 512, 512], P('energy', 'momentum')
- retarded_new: bfloat16 [8, 4, 2, 512, 512], P('energy', 'momentum')
Inputs may be any that keep to these rules, and one draw needn't show every extreme that they name: The energies of the grid are held in slots in an order of their own, one energy a slot. Mode m has one shift, the same for all slots: shift_slots[m, 0, j] is the slot of the energy that lies that shift below the energy of slot j, shift_slots[m, 1, j] the slot of the energy as far above it, and 8 where that energy lies outside the grid.
All inputs are finite; a program needn't handle non-finite values.
Results may differ from a plain program's by a relative error of at most 0.0064.
Values may be sent and summed in bfloat16 or wider, within the bound.
A program may use at most 64 MiB of HBM per device.

v0:
```python
import jax
import jax.numpy as jnp
from jax import lax
from jax.sharding import PartitionSpec as P


def matrix_product(former, latter):
    return jnp.matmul(former, latter, preferred_element_type=jnp.float32)


def complex_product(former, latter):
    former_re = former[..., 0, :, :]
    former_im = former[..., 1, :, :]
    latter_re = latter[..., 0, :, :]
    latter_im = latter[..., 1, :, :]
    real_part = matrix_product(former_re, latter_re) - matrix_product(former_im, latter_im)
    imag_part = matrix_product(former_re, latter_im) + matrix_product(former_im, latter_re)
    return jnp.stack([real_part, imag_part], axis=-3)


def adjoint_product(former, propagator):
    former_re = former[..., 0, :, :]
    former_im = former[..., 1, :, :]
    prop_re = jnp.swapaxes(propagator[..., 0, :, :], -1, -2)
    prop_im = jnp.swapaxes(propagator[..., 1, :, :], -1, -2)
    real_part = matrix_product(former_re, prop_re) + matrix_product(former_im, prop_im)
    imag_part = matrix_product(former_im, prop_re) - matrix_product(former_re, prop_im)
    return jnp.stack([real_part, imag_part], axis=-3)


def scattering(less_part, more_part, weights, occupation, shift_slots):
    slots = less_part.shape[0]
    slot_ids = jnp.arange(slots, dtype=jnp.int32)
    picked = (shift_slots[..., None] == slot_ids).astype(jnp.float32)
    phonons = occupation[:, None, None]
    pick_less = phonons * picked[:, 0] + (phonons + 1.0) * picked[:, 1]
    pick_more = (phonons + 1.0) * picked[:, 0] + phonons * picked[:, 1]
    mixer_less = jnp.einsum("mjs,mkq->jksq", pick_less, weights, precision=lax.Precision.HIGHEST)
    mixer_more = jnp.einsum("mjs,mkq->jksq", pick_more, weights, precision=lax.Precision.HIGHEST)
    total_less = jnp.einsum(
        "jksq,sqxab->jkxab",
        mixer_less,
        less_part.astype(jnp.float32),
        precision=lax.Precision.HIGHEST,
    )
    total_more = jnp.einsum(
        "jksq,sqxab->jkxab",
        mixer_more,
        more_part.astype(jnp.float32),
        precision=lax.Precision.HIGHEST,
    )
    return (total_less, total_more)


def per_device(lesser, greater, retarded, occupation, shift_slots, coupling):
    momenta = coupling.shape[1]
    modes = coupling.shape[0]
    order = lesser.shape[3]
    factor = 1.0 / (order * 4.0 * (modes * momenta) ** 0.5)
    weights = coupling.astype(jnp.float32)
    rows_less, rows_more = (
        lax.all_to_all(lesser, "energy", split_axis=3, concat_axis=0, tiled=True),
        lax.all_to_all(greater, "energy", split_axis=3, concat_axis=0, tiled=True),
    )
    own_index = lax.axis_index("momentum")
    pieces = (
        lax.all_gather(rows_less, "momentum", axis=1, tiled=True),
        lax.all_gather(rows_more, "momentum", axis=1, tiled=True),
    )
    count = pieces[0].shape[1]
    chosen = lax.dynamic_slice(weights, (0, own_index, 0), (modes, 1, count))
    add_less, add_more = scattering(pieces[0], pieces[1], chosen, occupation, shift_slots)
    sigma_less = (add_less * factor).astype(jnp.bfloat16)
    sigma_more = (add_more * factor).astype(jnp.bfloat16)
    sigma_less, sigma_more = (
        lax.all_to_all(sigma_less, "energy", split_axis=0, concat_axis=3, tiled=True),
        lax.all_to_all(sigma_more, "energy", split_axis=0, concat_axis=3, tiled=True),
    )
    sigma_ret = ((sigma_more.astype(jnp.float32) - sigma_less.astype(jnp.float32)) * 0.5).astype(
        jnp.bfloat16
    )
    stacked = jnp.stack([sigma_less, sigma_more, sigma_ret])
    halfway = complex_product(retarded[None], stacked).astype(jnp.bfloat16)
    lesser_new = adjoint_product(halfway[0], retarded).astype(jnp.bfloat16)
    greater_new = adjoint_product(halfway[1], retarded).astype(jnp.bfloat16)
    retarded_new = (retarded.astype(jnp.float32) + complex_product(halfway[2], retarded)).astype(
        jnp.bfloat16
    )
    return (lesser_new, greater_new, retarded_new)


def solution(mesh):
    return jax.shard_map(
        per_device,
        mesh=mesh,
        in_specs=(
            P("energy", "momentum", None, None, None),
            P("energy", "momentum", None, None, None),
            P("energy", "momentum", None, None, None),
            P(),
            P(),
            P(),
        ),
        out_specs=(
            P("energy", "momentum", None, None, None),
            P("energy", "momentum", None, None, None),
            P("energy", "momentum", None, None, None),
        ),
        check_vma=False,
    )
```

profile of v0, /device:TPU:0, one launch (start us, length us, event | category | flops | bytes accessed | tf_op | source)
XLA Modules:
  0.0 179.2 jit_solution(12115761878033358903)
XLA Ops:
  7.2 2.3 %copy.29 = bf16[1,1,2,512,512]{4,2,1,0,3:T(2,128)(2,1)S(1)} copy(bf16[1,1,2,512,512]{4,3,2,1,0:T(8,128)(2,1)} %param.6) | data formatting | bytes 2097152 | tf_op args[0]
  9.5 33.0 %all_to_all.66 = bf16[1,1,2,512,512]{4,2,1,0,3:T(2,128)(2,1)S(1)} all-to-all(bf16[1,1,2,512,512]{4,2,1,0,3:T(2,128)(2,1)S(1)} %copy.29), channel_id=1, replica_groups=mesh['energy'=8,'momentum'=4] {'energy'}, dimensions={3} | all-to-all | bytes 2097152 | tf_op jit(solution)/shard_map/all_to_all | solution.py:62
  42.5 1.5 copy.69
  44.1 1.1 copy.36
  45.3 28.8 %all_to_all.67 = bf16[1,1,2,512,512]{4,2,1,0,3:T(2,128)(2,1)S(1)} all-to-all(bf16[1,1,2,512,512]{4,2,1,0,3:T(2,128)(2,1)S(1)} %copy.36), channel_id=1, replica_groups=mesh['energy'=8,'momentum'=4] {'energy'}, dimensions={3} | all-to-all | bytes 2097152 | tf_op jit(solution)/shard_map/all_to_all | solution.py:63
  74.1 1.5 copy.68
  75.7 0.7 dynamic-slice_convert_fusion
  76.8 1.0 all-gather.5.cloned.1.call-done
  77.8 9.7 %fusion.15 = bf16[8,1,2,64,512]{4,0,3,2,1:T(8,128)(2,1)S(1)} fusion(bf16[8,4,1,2,64,512]{5,0,1,4,3,2:T(8,128)(2,1)} %all-gather.5.cloned.1.call-done, f32[8,8,4,1,1]{1,2,0,4,3:T(4,128)S(1)} %convolution_bitcast_fusion.1), kind=kOutput, calls=%fused_computation.24 | convolution fusion | flops 202375168 | bytes 5243904 | tf_op jit(solution)/shard_map/jksq,sqxab->jkxab/dot_general | solution.py:40
  87.4 1.3 copy.33
  88.7 5.5 %all-to-all-start.1 = ((bf16[8,1,2,64,512]{4,3,2,1,0:T(8,128)(2,1)}), bf16[8,1,2,64,512]{4,3,2,1,0:T(8,128)(2,1)S(1)}, u32[]{:S(2)}, u32[]{:S(2)}) async-start(bf16[8,1,2,64,512]{4,3,2,1,0:T(8,128)(2,1)} %copy.33), calls=%async_computation.1 | async-start | bytes 2097152 | tf_op jit(solution)/shard_map/all_to_all | solution.py:76
  94.4 20.0 %all-gather.7.cloned.1.call-done = bf16[8,4,1,2,64,512]{5,0,1,4,3,2:T(8,128)(2,1)} async-done(((bf16[8,1,1,2,64,512]{5,0,1,4,3,2:T(8,128)(2,1)}), bf16[8,4,1,2,64,512]{5,0,1,4,3,2:T(8,128)(2,1)}) %all-gather.7.cloned.1.call-update) | async-done | bytes 4194320 | tf_op jit(solution)/shard_map/all_gather | solution.py:68
  114.4 9.7 %fusion.18 = bf16[8,1,2,64,512]{4,0,3,2,1:T(8,128)(2,1)S(1)} fusion(bf16[8,4,1,2,64,512]{5,0,1,4,3,2:T(8,128)(2,1)} %all-gather.7.cloned.1.call-done, f32[8,8,4,1,1]{1,2,0,4,3:T(4,128)S(1)} %convolution_bitcast_fusion), kind=kOutput, calls=%fused_computation.25 | convolution fusion | flops 202375168 | bytes 5243904 | tf_op jit(solution)/shard_map/jksq,sqxab->jkxab/dot_general | solution.py:46
  124.0 1.3 copy.40
  125.3 5.5 %all-to-all-start.3 = ((bf16[8,1,2,64,512]{4,3,2,1,0:T(8,128)(2,1)}), bf16[8,1,2,64,512]{4,3,2,1,0:T(8,128)(2,1)S(1)}, u32[]{:S(2)}, u32[]{:S(2)}) async-start(bf16[8,1,2,64,512]{4,3,2,1,0:T(8,128)(2,1)} %copy.40), calls=%async_computation.3 | async-start | bytes 2097152 | tf_op jit(solution)/shard_map/all_to_all | solution.py:77
  131.5 25.5 %all-to-all-done.3 = bf16[8,1,2,64,512]{4,3,2,1,0:T(8,128)(2,1)S(1)} async-done(((bf16[8,1,2,64,512]{4,3,2,1,0:T(8,128)(2,1)}), bf16[8,1,2,64,512]{4,3,2,1,0:T(8,128)(2,1)S(1)}, u32[]{:S(2)}, u32[]{:S(2)}) %all-to-all-start.3) | async-done | bytes 1048608 | tf_op jit(solution)/shard_map/all_to_all | solution.py:77
  157.1 0.5 copy.45
  158.4 0.9 copy-done
  159.2 1.0 fusion.14
  160.2 1.0 fusion.13
  161.3 1.1 fusion.12
  162.3 1.1 fusion.11
  169.5 1.4 fusion.4
  170.8 1.5 pad_maximum_fusion.2
  (36 shorter events, 8.1 us)
Async XLA Ops:
  7.2 70.6 %all-gather.5.cloned.1.call-start = ((), (), s32[]{:S(2)}) async-start(), calls=%async_computation.4 | async-start | bytes 5242880 | tf_op jit(solution)/shard_map/all_gather | solution.py:67
  9.5 34.6 %copy-start.1 = (bf16[1,1,2,512,512]{4,3,2,1,0:T(8,128)(2,1)S(1)}, bf16[1,1,2,512,512]{4,3,2,1,0:T(8,128)(2,1)}, u32[]{:S(2)}) copy-start(bf16[1,1,2,512,512]{4,3,2,1,0:T(8,128)(2,1)} %param.7) | copy-start | bytes 3145732
  44.1 70.3 %all-gather.7.cloned.1.call-start = ((), (), s32[]{:S(2)}) async-start(), calls=%async_computation.5 | async-start | bytes 5242880 | tf_op jit(solution)/shard_map/all_gather | solution.py:68
  45.2 30.5 %copy-start.2 = (s32[2,2,8]{2,1,0:T(2,128)S(1)}, s32[2,2,8]{2,1,0:T(2,128)}, u32[]{:S(2)}) copy-start(s32[2,2,8]{2,1,0:T(2,128)} %param.10) | copy-start | bytes 388
  45.2 31.2 %copy-start.3 = (f32[2]{0:T(128)S(1)}, f32[2]{0:T(128)}, u32[]{:S(2)}) copy-start(f32[2]{0:T(128)} %param.9) | copy-start | bytes 28
  88.7 36.6 %all-to-all-start.1 = ((bf16[8,1,2,64,512]{4,3,2,1,0:T(8,128)(2,1)}), bf16[8,1,2,64,512]{4,3,2,1,0:T(8,128)(2,1)S(1)}, u32[]{:S(2)}, u32[]{:S(2)}) async-start(bf16[8,1,2,64,512]{4,3,2,1,0:T(8,128)(2,1)} %copy.33), calls=%async_computation.1 | async-start | bytes 2097152 | tf_op jit(solution)/shard_map/all_to_all | solution.py:76
  125.3 31.7 %all-to-all-start.3 = ((bf16[8,1,2,64,512]{4,3,2,1,0:T(8,128)(2,1)}), bf16[8,1,2,64,512]{4,3,2,1,0:T(8,128)(2,1)S(1)}, u32[]{:S(2)}, u32[]{:S(2)}) async-start(bf16[8,1,2,64,512]{4,3,2,1,0:T(8,128)(2,1)} %copy.40), calls=%async_computation.3 | async-start | bytes 2097152 | tf_op jit(solution)/shard_map/all_to_all | solution.py:77
  158.0 1.2 copy-start
Sparse Core Ops, SparseCore 0:
  44.2 33.5 all-gather.4
  79.9 34.4 all-gather.6
where the time goes:
time: 180 us; the launch traced here: 179 us
  blocking collectives  61.8 us (34%)
  waiting for transfers between devices  46.5 us (26%)
  matrix products  29.6 us (16%)
  between operations  14.3 us (8%)
  local copies, waits for them, and re-layouts  11.2 us (6%)
  starting transfers between devices  11.1 us (6%)
  other arithmetic  4.65 us (3%)
    all_to_all x1, blocking collectives, per_device(): lax.all_to_all(lesser, 'energy', split_axis=3, concat_axis=0, tiled=True)  33 us
    all_to_all x1, blocking collectives, per_device(): lax.all_to_all(greater, 'energy', split_axis=3, concat_axis=0, tiled=True)  28.8 us
    all_to_all x1, waiting for transfers between devices, per_device(): lax.all_to_all(sigma_more, 'energy', split_axis=0, concat_axis=3, tiled=T...  25.5 us
    all_gather x1, waiting for transfers between devices, per_device(): lax.all_gather(rows_more, 'momentum', axis=1, tiled=True)  20 us
    dot_general x16, matrix products, matrix_product(): return jnp.matmul(former, latter, preferred_element_type=jnp.float32)  9.88 us
    dot_general x1, matrix products, scattering(): jnp.einsum('jksq,sqxab->jkxab', mixer_less, less_part.astype(jnp.float32)...  9.66 us
    dot_general x1, matrix products, scattering(): jnp.einsum('jksq,sqxab->jkxab', mixer_more, more_part.astype(jnp.float32)...  9.66 us
    all_to_all x1, starting transfers between devices, per_device(): lax.all_to_all(sigma_more, 'energy', split_axis=0, concat_axis=3, tiled=T...  5.52 us
  transfers between devices with their start and end apart: 4, of which 3 were waited for; matrix products, arithmetic and copies ran while one was open for 15% of the time, Pallas kernels for 0%

commit v1 on v0

v1 whole, which is shorter than its diff:
```python
import functools

import jax
import jax.numpy as jnp
from jax import lax
from jax.experimental import pallas as pl
from jax.experimental.pallas import tpu as pltpu
from jax.sharding import PartitionSpec as P

MESH = pl.DeviceIdType.MESH


def dot(a, b):
    return jnp.dot(a, b, preferred_element_type=jnp.float32)


def dot_t(a, b):
    return lax.dot_general(a, b, (((1,), (1,)), ((), ())), preferred_element_type=jnp.float32)


def kernel(
    sizes,
    factor,
    less_ref,
    more_ref,
    ret_ref,
    occ_ref,
    shift_ref,
    coup_ref,
    less_out,
    more_out,
    ret_out,
    recv_less,
    recv_more,
    mixed,
    send_less,
    send_more,
    sig_less,
    sig_more,
    half,
    send_sem,
    recv_sem,
    own_sem,
):
    energies, momenta, modes, parts, rows, cols, row_groups, col_groups = sizes
    n = energies * momenta
    my_e, my_m = lax.axis_index("energy"), lax.axis_index("momentum")
    me = my_e * momenta + my_m
    order = row_groups * rows

    def partner(i):
        t = i // momenta
        up = energies // 2 + t // 2
        down = energies // 2 - (t + 1) // 2
        offset = up + (t % 2) * (down - up)
        e = lax.rem(my_e + offset, energies)
        m = lax.rem(my_m + i % momenta + 1, momenta)
        return e, m

    def piece(ref, lead, d):
        row = pl.multiple_of(lax.rem(d, row_groups) * rows, rows)
        rest = d // row_groups
        col = pl.multiple_of(lax.rem(rest, col_groups) * cols, cols)
        part = (rest // col_groups) * parts
        index = (pl.ds(part, parts), pl.ds(row, rows), pl.ds(col, cols))
        return ref.at[(0,) * lead + index]

    barrier = pltpu.get_barrier_semaphore()

    def greet(i, carry):
        pl.semaphore_signal(barrier, inc=1, device_id=partner(i), device_id_type=MESH)
        return carry

    lax.fori_loop(0, n - 1, greet, 0)
    own_less = pltpu.make_async_copy(piece(less_ref, 2, me), recv_less.at[me], own_sem.at[0])
    own_more = pltpu.make_async_copy(piece(more_ref, 2, me), recv_more.at[me], own_sem.at[1])
    own_less.start()
    own_more.start()
    pl.semaphore_wait(barrier, n - 1)

    def forward(ref, landing, which):
        def send(i, carry):
            e, m = partner(i)
            pltpu.make_async_remote_copy(
                src_ref=piece(ref, 2, e * momenta + m),
                dst_ref=landing.at[me],
                send_sem=send_sem.at[which],
                recv_sem=recv_sem.at[which],
                device_id=(e, m),
                device_id_type=MESH,
            ).start()
            return carry

        lax.fori_loop(0, n - 1, send, 0)

    def back(ref, landing, which):
        def send(i, carry):
            e, m = partner(i)
            pltpu.make_async_remote_copy(
                src_ref=ref.at[e * momenta + m],
                dst_ref=piece(landing, 0, me),
                send_sem=send_sem.at[which],
                recv_sem=recv_sem.at[which],
                device_id=(e, m),
                device_id_type=MESH,
            ).start()
            return carry

        lax.fori_loop(0, n - 1, send, 0)

    def wait_all(sem):
        span = recv_less.at[pl.ds(0, n - 1)]
        pltpu.make_async_copy(span, span, sem).wait()

    forward(less_ref, recv_less, 0)
    forward(more_ref, recv_more, 1)

    mixed[:, energies] = jnp.zeros((modes, momenta, parts, rows, cols), jnp.float32)
    width = min(cols, 256)
    blocks = parts * (cols // width)

    def mix(recv, send, add_below, add_above):
        def over_momenta(i, carry):
            s, b = i // blocks, i % blocks
            part = b // (cols // width)
            at = pl.ds(pl.multiple_of((b % (cols // width)) * width, width), width)
            terms = [recv[s * momenta + q, part, :, at].astype(jnp.float32) for q in range(momenta)]
            for m in range(modes):
                for k in range(momenta):
                    total = coup_ref[m, k, 0].astype(jnp.float32) * terms[0]
                    for q in range(1, momenta):
                        total += coup_ref[m, k, q].astype(jnp.float32) * terms[q]
                    mixed[m, s, k, part, :, at] = total
            return carry

        lax.fori_loop(0, energies * blocks, over_momenta, 0)

        def over_energies(i, carry):
            j, b = i // blocks, i % blocks
            part = b // (cols // width)
            at = pl.ds(pl.multiple_of((b % (cols // width)) * width, width), width)
            for k in range(momenta):
                total = None
                for m in range(modes):
                    phonons = occ_ref[m]
                    for side, add in ((0, add_below), (1, add_above)):
                        term = ((phonons + add) * factor) * mixed[m, shift_ref[m, side, j], k, part, :, at]
                        total = term if total is None else total + term
                send[j * momenta + k, part, :, at] = total.astype(jnp.bfloat16)
            return carry

        lax.fori_loop(0, energies * blocks, over_energies, 0)

    tile = min(order, 256)

    def halfway(sigma_of):
        def step(i, carry):
            at = pl.ds(pl.multiple_of(i * tile, tile), tile)
            re, im = sigma_of(0, at), sigma_of(1, at)
            ret_re, ret_im = ret_ref[0, 0, 0], ret_ref[0, 0, 1]
            half[0, :, at] = (dot(ret_re, re) - dot(ret_im, im)).astype(jnp.bfloat16)
            half[1, :, at] = (dot(ret_re, im) + dot(ret_im, re)).astype(jnp.bfloat16)
            return carry

        lax.fori_loop(0, order // tile, step, 0)

    def adjoint(out):
        def step(i, carry):
            at = pl.ds(pl.multiple_of(i * tile, tile), tile)
            ret_re, ret_im = ret_ref[0, 0, 0, at], ret_ref[0, 0, 1, at]
            re, im = half[0], half[1]
            out[0, 0, 0, :, at] = (dot_t(re, ret_re) + dot_t(im, ret_im)).astype(jnp.bfloat16)
            out[0, 0, 1, :, at] = (dot_t(im, ret_re) - dot_t(re, ret_im)).astype(jnp.bfloat16)
            return carry

        lax.fori_loop(0, order // tile, step, 0)

    own_less.wait()
    wait_all(recv_sem.at[0])
    mix(recv_less, send_less, 0.0, 1.0)
    back(send_less, sig_less, 2)
    keep_less = pltpu.make_async_copy(send_less.at[me], piece(sig_less, 0, me), own_sem.at[0])
    keep_less.start()

    own_more.wait()
    wait_all(recv_sem.at[1])
    mix(recv_more, send_more, 1.0, 0.0)
    back(send_more, sig_more, 3)
    keep_more = pltpu.make_async_copy(send_more.at[me], piece(sig_more, 0, me), own_sem.at[1])
    keep_more.start()

    keep_less.wait()
    wait_all(recv_sem.at[2])
    halfway(lambda x, at: sig_less[x, :, at])
    adjoint(less_out)

    keep_more.wait()
    wait_all(recv_sem.at[3])
    halfway(lambda x, at: sig_more[x, :, at])
    adjoint(more_out)

    def sigma_ret(x, at):
        more = sig_more[x, :, at].astype(jnp.float32)
        less = sig_less[x, :, at].astype(jnp.float32)
        return ((more - less) * 0.5).astype(jnp.bfloat16)

    halfway(sigma_ret)

    def dyson(i, carry):
        at = pl.ds(pl.multiple_of(i * tile, tile), tile)
        ret_re, ret_im = ret_ref[0, 0, 0, :, at], ret_ref[0, 0, 1, :, at]
        re, im = half[0], half[1]
        ret_out[0, 0, 0, :, at] = (
            ret_re.astype(jnp.float32) + (dot(re, ret_re) - dot(im, ret_im))
        ).astype(jnp.bfloat16)
        ret_out[0, 0, 1, :, at] = (
            ret_im.astype(jnp.float32) + (dot(re, ret_im) + dot(im, ret_re))
        ).astype(jnp.bfloat16)
        return carry

    lax.fori_loop(0, order // tile, dyson, 0)
    for which in range(4):
        wait_all(send_sem.at[which])


def per_device(energies, momenta, lesser, greater, retarded, occupation, shift_slots, coupling):
    n = energies * momenta
    modes = coupling.shape[0]
    order = lesser.shape[-1]
    factor = 1.0 / (order * 4.0 * (modes * momenta) ** 0.5)
    row_groups = min(n, order // 16)
    col_groups = min(n // row_groups, order // 128)
    part_groups = n // (row_groups * col_groups)
    parts, rows, cols = 2 // part_groups, order // row_groups, order // col_groups
    sizes = (energies, momenta, modes, parts, rows, cols, row_groups, col_groups)
    vmem = pl.BlockSpec(memory_space=pltpu.VMEM)
    smem = pl.BlockSpec(memory_space=pltpu.SMEM)
    hbm = pl.BlockSpec(memory_space=pl.ANY)
    exchanged = pltpu.VMEM((n, parts, rows, cols), jnp.bfloat16)
    block = pltpu.VMEM((2, order, order), jnp.bfloat16)
    return pl.pallas_call(
        functools.partial(kernel, sizes, factor),
        out_shape=tuple(jax.ShapeDtypeStruct(lesser.shape, jnp.bfloat16) for _ in range(3)),
        in_specs=[hbm, hbm, vmem, smem, smem, smem],
        out_specs=(vmem, vmem, vmem),
        scratch_shapes=[
            exchanged,
            exchanged,
            pltpu.VMEM((modes, energies + 1, momenta, parts, rows, cols), jnp.float32),
            exchanged,
            exchanged,
            block,
            block,
            block,
            pltpu.SemaphoreType.DMA((4,)),
            pltpu.SemaphoreType.DMA((4,)),
            pltpu.SemaphoreType.DMA((2,)),
        ],
        compiler_params=pltpu.CompilerParams(
            collective_id=0, has_side_effects=True, vmem_limit_bytes=40 * 1024 * 1024
        ),
        cost_estimate=pl.CostEstimate(
            flops=48 * order**3, bytes_accessed=24 * order * order, transcendentals=0
        ),
    )(lesser, greater, retarded, occupation, shift_slots, coupling)


def solution(mesh):
    split = P("energy", "momentum", None, None, None)
    return jax.shard_map(
        functools.partial(per_device, mesh.shape["energy"], mesh.shape["momentum"]),
        mesh=mesh,
        in_specs=(split, split, split, P(), P(), P()),
        out_specs=(split, split, split),
        check_vma=False,
    )
```

time: 180 us -> 113 us (0.63)
  the two profiles are of different devices: /device:TPU:0 before, /device:TPU:12 now
where the time goes in v1:
time: 113 us; the launch traced here: 112 us
  Pallas kernels  103 us (91%)
  local copies, waits for them, and re-layouts  8.6 us (8%)
    pallas_call x1, Pallas kernels, per_device(): pl.pallas_call(functools.partial(kernel, sizes, factor), out_shape=tuple(...  103 us
    unnamed x15, local copies, waits for them, and re-layouts  8.6 us

profile of v1, /device:TPU:12, one launch (start us, length us, event | category | flops | bytes accessed | tf_op | source)
XLA Modules:
  0.0 112.2 jit_solution(2562623231824234953)
XLA Ops:
  0.6 0.0 copy-start
  0.6 1.2 %copy-done = bf16[1,1,2,512,512]{4,3,2,1,0:T(8,128)(2,1)S(1)} copy-done((bf16[1,1,2,512,512]{4,3,2,1,0:T(8,128)(2,1)S(1)}, bf16[1,1,2,512,512]{4,3,2,1,0:T(8,128)(2,1)}, u32[]{:S(2)}) %copy-start) | copy-done | bytes 1048600
  1.9 0.0 copy-start.1
  1.9 1.2 %copy-done.1 = bf16[1,1,2,512,512]{4,3,2,1,0:T(8,128)(2,1)S(1)} copy-done((bf16[1,1,2,512,512]{4,3,2,1,0:T(8,128)(2,1)S(1)}, bf16[1,1,2,512,512]{4,3,2,1,0:T(8,128)(2,1)}, u32[]{:S(2)}) %copy-start.1) | copy-done | bytes 1048600
  3.1 0.0 copy-start.2
  3.1 1.2 %copy-done.2 = bf16[1,1,2,512,512]{4,3,2,1,0:T(8,128)(2,1)S(1)} copy-done((bf16[1,1,2,512,512]{4,3,2,1,0:T(8,128)(2,1)S(1)}, bf16[1,1,2,512,512]{4,3,2,1,0:T(8,128)(2,1)}, u32[]{:S(2)}) %copy-start.2) | copy-done | bytes 1048600
  4.3 0.0 copy-start.3
  4.3 0.7 copy-done.3
  5.0 0.0 copy-start.4
  5.0 0.7 copy-done.4
  5.7 0.0 copy-start.5
  5.7 0.7 copy-done.5
  6.3 103.0 %shard_map.85 = (bf16[1,1,2,512,512]{4,3,2,1,0:T(8,128)(2,1)S(1)}, bf16[1,1,2,512,512]{4,3,2,1,0:T(8,128)(2,1)S(1)}, bf16[1,1,2,512,512]{4,3,2,1,0:T(8,128)(2,1)S(1)}) custom-call(bf16[1,1,2,512,512]{4,3,2,1,0:T(8,128)(2,1)S(1)} %copy-done, bf16[1,1,2,512,512]{4,3,2,1,0:T(8,128)(2,1)S(1)} %copy-done.1, bf16[1,1,2,512,512]{4,3,2,1,0:T(8,128)(2,1)S(1)} %copy-done.2, ...), custom_call_target="tpu_custom_call" | custom-call | flops 6442450944 | bytes 6291456 | tf_op jit(solution)/shard_map/pallas_call | solution.py:241
  109.3 1.0 copy.12
  110.3 1.0 copy.13
  111.2 1.0 copy.14
Async XLA Ops:
  0.6 1.2 %copy-start = (bf16[1,1,2,512,512]{4,3,2,1,0:T(8,128)(2,1)S(1)}, bf16[1,1,2,512,512]{4,3,2,1,0:T(8,128)(2,1)}, u32[]{:S(2)}) copy-start(bf16[1,1,2,512,512]{4,3,2,1,0:T(8,128)(2,1)} %less_ref.1) | copy-start | bytes 3145732
  1.9 1.2 %copy-start.1 = (bf16[1,1,2,512,512]{4,3,2,1,0:T(8,128)(2,1)S(1)}, bf16[1,1,2,512,512]{4,3,2,1,0:T(8,128)(2,1)}, u32[]{:S(2)}) copy-start(bf16[1,1,2,512,512]{4,3,2,1,0:T(8,128)(2,1)} %more_ref.1) | copy-start | bytes 3145732
  3.1 1.2 %copy-start.2 = (bf16[1,1,2,512,512]{4,3,2,1,0:T(8,128)(2,1)S(1)}, bf16[1,1,2,512,512]{4,3,2,1,0:T(8,128)(2,1)}, u32[]{:S(2)}) copy-start(bf16[1,1,2,512,512]{4,3,2,1,0:T(8,128)(2,1)} %ret_ref.1) | copy-start | bytes 3145732
  4.3 0.7 copy-start.3
  5.0 0.7 copy-start.4
  5.7 0.7 copy-start.5

commit v2 on v1

v2 whole, which is shorter than its diff:
```python
import functools

import jax
import jax.numpy as jnp
from jax import lax
from jax.experimental import pallas as pl
from jax.experimental.pallas import tpu as pltpu
from jax.sharding import PartitionSpec as P

MESH = pl.DeviceIdType.MESH


def dot(a, b):
    return jnp.dot(a, b, preferred_element_type=jnp.float32)


def dot_t(a, b):
    return lax.dot_general(a, b, (((1,), (1,)), ((), ())), preferred_element_type=jnp.float32)


def kernel(
    sizes,
    factor,
    less_ref,
    more_ref,
    ret_ref,
    occ_ref,
    shift_ref,
    coup_ref,
    less_out,
    more_out,
    ret_out,
    ret_held,
    occ_held,
    shift_held,
    coup_held,
    recv_less,
    recv_more,
    mixed,
    send_less,
    send_more,
    sig_less,
    sig_more,
    half,
    half_ret,
    half_less,
    sum_more,
    sum_ret,
    send_sem,
    recv_sem,
    own_sem,
    load_sem,
):
    energies, momenta, modes, parts, rows, cols, row_groups, col_groups = sizes
    n = energies * momenta
    my_e, my_m = lax.axis_index("energy"), lax.axis_index("momentum")
    me = my_e * momenta + my_m
    order = row_groups * rows

    pieces = max(cols // 256, 1)
    width = cols // pieces

    my_row = [lax.rem(my_m + m + 1, momenta) for m in range(momenta)]

    def others(act):
        def at_energy(t, carry):
            odd = lax.rem(t, 2)
            half_t = lax.div(t + odd, 2)
            offset = energies // 2 + half_t - 2 * odd * half_t
            e = lax.rem(my_e + offset, energies)
            for m in my_row:
                act(e, m)
            return carry

        lax.fori_loop(0, energies - 1, at_energy, 0)
        for m in my_row[:-1]:
            act(my_e, m)

    def piece(ref, lead, d, begin, count):
        row = pl.multiple_of(lax.rem(d, row_groups) * rows, rows)
        rest = lax.div(d, row_groups)
        col = pl.multiple_of(lax.rem(rest, col_groups) * cols, cols) + begin
        part = lax.div(rest, col_groups) * parts
        index = (pl.ds(part, parts), pl.ds(row, rows), pl.ds(col, count))
        return ref.at[(0,) * lead + index]

    barrier = pltpu.get_barrier_semaphore()

    def greet(e, m):
        pl.semaphore_signal(barrier, inc=1, device_id=(e, m), device_id_type=MESH)

    others(greet)
    loads = [
        pltpu.make_async_copy(piece(less_ref, 2, me, 0, cols), recv_less.at[me], own_sem.at[0]),
        pltpu.make_async_copy(piece(more_ref, 2, me, 0, cols), recv_more.at[me], own_sem.at[1]),
        pltpu.make_async_copy(ret_ref, ret_held, load_sem.at[0]),
        pltpu.make_async_copy(occ_ref, occ_held, load_sem.at[1]),
        pltpu.make_async_copy(shift_ref, shift_held, load_sem.at[2]),
        pltpu.make_async_copy(coup_ref, coup_held, load_sem.at[3]),
    ]
    for load in loads:
        load.start()
    pl.semaphore_wait(barrier, n - 1)

    def forward(ref, landing, which):
        def send(e, m):
            pltpu.make_async_remote_copy(
                src_ref=piece(ref, 2, e * momenta + m, 0, cols),
                dst_ref=landing.at[me],
                send_sem=send_sem.at[which],
                recv_sem=recv_sem.at[which],
                device_id=(e, m),
                device_id_type=MESH,
            ).start()

        others(send)

    def back(ref, landing, begin, count, which):
        def send(e, m):
            pltpu.make_async_remote_copy(
                src_ref=ref.at[e * momenta + m, :, :, pl.ds(begin, count)],
                dst_ref=piece(landing, 0, me, begin, count),
                send_sem=send_sem.at[which],
                recv_sem=recv_sem.at[which],
                device_id=(e, m),
                device_id_type=MESH,
            ).start()

        others(send)

    def wait_all(sem, count):
        span = recv_less.at[pl.ds(0, n - 1), :, :, pl.ds(0, count)]
        pltpu.make_async_copy(span, span, sem).wait()

    forward(less_ref, recv_less, 0)
    forward(more_ref, recv_more, 1)

    mixed[:, energies] = jnp.zeros((modes, momenta, parts, rows, cols), jnp.float32)

    def mix(recv, send, add_below, add_above, begin, count):
        step = min(count, 256)
        blocks = parts * (count // step)

        def place(i):
            b = lax.rem(i, blocks)
            col = begin + lax.rem(b, count // step) * step
            at = pl.ds(pl.multiple_of(col, step), step)
            return lax.div(i, blocks), lax.div(b, count // step), at

        def over_momenta(i, carry):
            s, part, at = place(i)
            terms = [recv[s * momenta + q, part, :, at].astype(jnp.float32) for q in range(momenta)]
            for m in range(modes):
                for k in range(momenta):
                    total = coup_held[m, k, 0].astype(jnp.float32) * terms[0]
                    for q in range(1, momenta):
                        total += coup_held[m, k, q].astype(jnp.float32) * terms[q]
                    mixed[m, s, k, part, :, at] = total
            return carry

        lax.fori_loop(0, energies * blocks, over_momenta, 0)

        def over_energies(i, carry):
            j, part, at = place(i)
            for k in range(momenta):
                total = None
                for m in range(modes):
                    phonons = occ_held[m]
                    for side, add in ((0, add_below), (1, add_above)):
                        term = ((phonons + add) * factor) * mixed[m, shift_held[m, side, j], k, part, :, at]
                        total = term if total is None else total + term
                send[j * momenta + k, part, :, at] = total.astype(jnp.bfloat16)
            return carry

        lax.fori_loop(0, energies * blocks, over_energies, 0)

    for load in loads[2:]:
        load.wait()
    loads[0].wait()
    wait_all(recv_sem.at[0], cols)
    mix(recv_less, send_less, 0.0, 1.0, 0, cols)
    back(send_less, sig_less, 0, cols, 2)
    keep_less = pltpu.make_async_copy(send_less.at[me], piece(sig_less, 0, me, 0, cols), own_sem.at[0])
    keep_less.start()

    loads[1].wait()
    wait_all(recv_sem.at[1], cols)
    keeps = []
    for c in range(pieces):
        begin = c * width
        mix(recv_more, send_more, 1.0, 0.0, begin, width)
        back(send_more, sig_more, begin, width, 3 + c)
        keep = pltpu.make_async_copy(
            send_more.at[me, :, :, pl.ds(begin, width)],
            piece(sig_more, 0, me, begin, width),
            own_sem.at[1 + c],
        )
        keep.start()
        keeps.append(keep)

    ret_re, ret_im = ret_held.at[0, 0, 0], ret_held.at[0, 0, 1]

    def halfway(sigma, at):
        re, im = sigma[0, :, at], sigma[1, :, at]
        left_re, left_im = ret_re[...], ret_im[...]
        return (
            dot(left_re, re) - dot(left_im, im),
            dot(left_re, im) + dot(left_im, re),
        )

    def adjoint(which, at, to):
        re, im = half[0, :, at], half[1, :, at]
        right_re, right_im = ret_re[to, at], ret_im[to, at]
        if which == 0:
            return dot_t(re, right_re) + dot_t(im, right_im)
        return dot_t(im, right_re) - dot_t(re, right_im)

    def dyson(which, at, to):
        re, im = half_ret[0, :, at], half_ret[1, :, at]
        right_re, right_im = ret_re[at, to], ret_im[at, to]
        if which == 0:
            return dot(re, right_re) - dot(im, right_im)
        return dot(re, right_im) + dot(im, right_re)

    tile = min(order, 256)
    tiles = [pl.ds(t * tile, tile) for t in range(order // tile)]

    keep_less.wait()
    wait_all(recv_sem.at[2], cols)
    for at in tiles:
        re, im = halfway(sig_less, at)
        half_less[0, :, at] = re
        half_less[1, :, at] = im
        half[0, :, at] = re.astype(jnp.bfloat16)
        half[1, :, at] = im.astype(jnp.bfloat16)
    for to in tiles:
        for x in range(2):
            less_out[0, 0, x, :, to] = adjoint(x, pl.ds(0, order), to).astype(jnp.bfloat16)

    stages = pieces if col_groups == 1 else 1
    span = order // stages
    for c in range(pieces):
        keeps[c].wait()
        wait_all(recv_sem.at[3 + c], width)
        if stages == 1 and c < pieces - 1:
            continue
        stage = c if stages > 1 else 0
        last = stage == stages - 1
        for t in range(span // tile):
            at = pl.ds(stage * span + t * tile, tile)
            for x, value in enumerate(halfway(sig_more, at)):
                half[x, :, at] = value.astype(jnp.bfloat16)
                half_ret[x, :, at] = ((value - half_less[x, :, at]) * 0.5).astype(jnp.bfloat16)
        at = pl.ds(stage * span, span)
        for to in tiles:
            for x in range(2):
                more, ret = adjoint(x, at, to), dyson(x, at, to)
                if stage > 0:
                    more += sum_more[x, :, to]
                    ret += sum_ret[x, :, to]
                if last:
                    more_out[0, 0, x, :, to] = more.astype(jnp.bfloat16)
                    ret += (ret_re, ret_im)[x][:, to].astype(jnp.float32)
                    ret_out[0, 0, x, :, to] = ret.astype(jnp.bfloat16)
                else:
                    sum_more[x, :, to] = more
                    sum_ret[x, :, to] = ret
    for which in range(3):
        wait_all(send_sem.at[which], cols)
    for c in range(pieces):
        wait_all(send_sem.at[3 + c], width)


def per_device(energies, momenta, lesser, greater, retarded, occupation, shift_slots, coupling):
    n = energies * momenta
    modes = coupling.shape[0]
    order = lesser.shape[-1]
    factor = 1.0 / (order * 4.0 * (modes * momenta) ** 0.5)
    row_groups = min(n, order // 16)
    col_groups = min(n // row_groups, order // 128)
    part_groups = n // (row_groups * col_groups)
    parts, rows, cols = 2 // part_groups, order // row_groups, order // col_groups
    sizes = (energies, momenta, modes, parts, rows, cols, row_groups, col_groups)
    vmem = pl.BlockSpec(memory_space=pltpu.VMEM)
    hbm = pl.BlockSpec(memory_space=pltpu.HBM)
    pieces = max(cols // 256, 1)
    exchanged = pltpu.VMEM((n, parts, rows, cols), jnp.bfloat16)
    block = pltpu.VMEM((2, order, order), jnp.bfloat16)
    wide = pltpu.VMEM((2, order, order), jnp.float32)
    return pl.pallas_call(
        functools.partial(kernel, sizes, factor),
        out_shape=tuple(jax.ShapeDtypeStruct(lesser.shape, jnp.bfloat16) for _ in range(3)),
        in_specs=[hbm] * 6,
        out_specs=(vmem, vmem, vmem),
        scratch_shapes=[
            pltpu.VMEM(retarded.shape, jnp.bfloat16),
            pltpu.SMEM(occupation.shape, jnp.float32),
            pltpu.SMEM(shift_slots.shape, jnp.int32),
            pltpu.SMEM(coupling.shape, jnp.int32),
            exchanged,
            exchanged,
            pltpu.VMEM((modes, energies + 1, momenta, parts, rows, cols), jnp.float32),
            exchanged,
            exchanged,
            block,
            block,
            block,
            block,
            wide,
            wide,
            wide,
            pltpu.SemaphoreType.DMA((3 + pieces,)),
            pltpu.SemaphoreType.DMA((3 + pieces,)),
            pltpu.SemaphoreType.DMA((1 + pieces,)),
            pltpu.SemaphoreType.DMA((4,)),
        ],
        compiler_params=pltpu.CompilerParams(
            collective_id=0, has_side_effects=True, vmem_limit_bytes=56 * 1024 * 1024
        ),
        cost_estimate=pl.CostEstimate(
            flops=48 * order**3, bytes_accessed=24 * order * order, transcendentals=0
        ),
    )(lesser, greater, retarded, occupation, shift_slots, coupling)


def solution(mesh):
    split = P("energy", "momentum", None, None, None)
    return jax.shard_map(
        functools.partial(per_device, mesh.shape["energy"], mesh.shape["momentum"]),
        mesh=mesh,
        in_specs=(split, split, split, P(), P(), P()),
        out_specs=(split, split, split),
        check_vma=False,
    )
```

time: 113 us -> 106 us (0.938)
  local copies, waits for them, and re-layouts: 8.6 us -> 4.93 us
  Pallas kernels: 103 us -> 100 us
    unnamed x15 -> x7, local copies, waits for them, and re-layouts: 8.6 us -> 4.93 us
    pallas_call x1, Pallas kernels: 103 us -> 100 us  [per_device(): pl.pallas_call(functools.partial(kernel, sizes, factor), out_shape=tuple(...]
where the time goes in v2:
time: 106 us
  Pallas kernels  100 us (94%)
  local copies, waits for them, and re-layouts  4.93 us (5%)
    pallas_call x1, Pallas kernels, per_device(): pl.pallas_call(functools.partial(kernel, sizes, factor), out_shape=tuple(...  100 us
    unnamed x7, local copies, waits for them, and re-layouts  4.93 us

profile of v2, /device:TPU:12, one launch (start us, length us, event | category | flops | bytes accessed | tf_op | source)
XLA Modules:
  0.0 106.0 jit_solution(9694803862889085100)
XLA Ops:
  0.6 100.5 %shard_map.85 = (bf16[1,1,2,512,512]{4,3,2,1,0:T(8,128)(2,1)}, bf16[1,1,2,512,512]{4,3,2,1,0:T(8,128)(2,1)}, bf16[1,1,2,512,512]{4,3,2,1,0:T(8,128)(2,1)}) custom-call(bf16[1,1,2,512,512]{4,3,2,1,0:T(8,128)(2,1)} %less_ref.1, bf16[1,1,2,512,512]{4,3,2,1,0:T(8,128)(2,1)} %more_ref.1, bf16[1,1,2,512,512]{4,3,2,1,0:T(8,128)(2,1)} %ret_ref.1, f32[2]{0:T(128)} %occ_ref.1, ...), custom_call_target="tpu_custom_call" | custom-call | flops 6442450944 | bytes 6291456 | tf_op jit(solution)/shard_map/pallas_call | solution.py:290
  101.1 0.0 copy-start.1
  101.1 2.4 %copy.12 = bf16[1,1,2,512,512]{4,3,2,1,0:T(8,128)(2,1)} copy(bf16[1,1,2,512,512]{4,3,2,1,0:T(8,128)(2,1)} %get-tuple-element.6) | data formatting | bytes 2097152
  103.5 0.0 copy-done.1
  103.5 0.0 copy-start
  103.5 1.0 copy.13
  104.4 0.6 copy-done
  105.1 1.0 copy.14
Async XLA Ops:
  101.1 2.4 %copy-start.1 = (bf16[1,1,2,512,512]{4,3,2,1,0:T(8,128)(2,1)S(1)}, bf16[1,1,2,512,512]{4,3,2,1,0:T(8,128)(2,1)}, u32[]{:S(2)}) copy-start(bf16[1,1,2,512,512]{4,3,2,1,0:T(8,128)(2,1)} %get-tuple-element.7) | copy-start | bytes 3145732
  103.5 1.6 %copy-start = (bf16[1,1,2,512,512]{4,3,2,1,0:T(8,128)(2,1)S(1)}, bf16[1,1,2,512,512]{4,3,2,1,0:T(8,128)(2,1)}, u32[]{:S(2)}) copy-start(bf16[1,1,2,512,512]{4,3,2,1,0:T(8,128)(2,1)} %get-tuple-element.8) | copy-start | bytes 3145732

commit v3 on v2

--- a/solution.py
+++ b/solution.py
@@ -315,7 +315,7 @@
             pltpu.SemaphoreType.DMA((4,)),
         ],
         compiler_params=pltpu.CompilerParams(
-            collective_id=0, has_side_effects=True, vmem_limit_bytes=56 * 1024 * 1024
+            collective_id=0, has_side_effects=True, vmem_limit_bytes=50 * 1024 * 1024
         ),
         cost_estimate=pl.CostEstimate(
             flops=48 * order**3, bytes_accessed=24 * order * order, transcendentals=0

time: 106 us -> 104 us (0.981)
  Pallas kernels: 100 us -> 98.7 us
    pallas_call x1, Pallas kernels: 100 us -> 98.7 us  [per_device(): pl.pallas_call(functools.partial(kernel, sizes, factor), out_shape=tuple(...]
    unnamed x7 -> x9, local copies, waits for them, and re-layouts: 4.93 us -> 4.93 us
where the time goes in v3:
time: 104 us
  Pallas kernels  98.7 us (95%)
  local copies, waits for them, and re-layouts  4.93 us (5%)
    pallas_call x1, Pallas kernels, per_device(): pl.pallas_call(functools.partial(kernel, sizes, factor), out_shape=tuple(...  98.7 us
    unnamed x9, local copies, waits for them, and re-layouts  4.93 us

profile of v3, /device:TPU:12, one launch (start us, length us, event | category | flops | bytes accessed | tf_op | source)
XLA Modules:
  0.0 104.3 jit_solution(4627601855361613323)
XLA Ops:
  0.6 0.0 copy-start
  0.6 0.7 copy-done
  1.3 0.0 copy-start.1
  1.3 0.7 copy-done.1
  2.0 0.0 copy-start.2
  2.0 0.7 copy-done.2
  2.7 98.7 %shard_map.85 = (bf16[1,1,2,512,512]{4,3,2,1,0:T(8,128)(2,1)S(1)}, bf16[1,1,2,512,512]{4,3,2,1,0:T(8,128)(2,1)S(1)}, bf16[1,1,2,512,512]{4,3,2,1,0:T(8,128)(2,1)S(1)}) custom-call(bf16[1,1,2,512,512]{4,3,2,1,0:T(8,128)(2,1)} %less_ref.1, bf16[1,1,2,512,512]{4,3,2,1,0:T(8,128)(2,1)} %more_ref.1, bf16[1,1,2,512,512]{4,3,2,1,0:T(8,128)(2,1)} %ret_ref.1, ...), custom_call_target="tpu_custom_call" | custom-call | flops 6442450944 | bytes 6291456 | tf_op jit(solution)/shard_map/pallas_call | solution.py:290
  101.3 1.0 copy.12
  102.3 1.0 copy.13
  103.3 1.0 copy.14
Async XLA Ops:
  0.6 0.7 copy-start
  1.3 0.7 copy-start.1
  2.0 0.7 copy-start.2
